TPU v7x, 512 devices: a whole 4x8x8 slice. The times are simulated.
512 devices in a mesh: sec: 2 (over core), grp: 16 (over y_hi, x), dev: 16 (over y_lo, z).
Axes of the slice: x: 4, y: 8 (y_hi: 4, y_lo: 2; y = y_hi * 2 + y_lo), z: 8, core: 2. Of those that a mesh axis runs over, the one named last changes fastest.
Arguments:
- q_latent: bfloat16 [256, 128, 512], P(('grp', 'dev')), may hold values from -16 to 16
- q_rope: bfloat16 [256, 8192], P(('grp', 'dev')), may hold values from -6 to 6
- cache_latent: bfloat16 [256, 2048, 512], P(('grp', 'dev'), 'sec'), may hold values from -6 to 6
- cache_rope: bfloat16 [256, 64, 2048], P(('grp', 'dev'), None, 'sec'), may hold values from -6 to 6
- lengths: int32 [256], P(('grp', 'dev')), may hold values from 2 to 2048
- w_uv: bfloat16 [128, 512, 128], P(('sec', 'grp')), may hold values from -1 to 1
- w_out: bfloat16 [16384, 7168], P(('sec', 'grp'), 'dev'), may hold values from -0.046875 to 0.046875
- resid: bfloat16 [256, 7168], P(('sec', 'grp'), 'dev'), may hold values from -6 to 6
- norm_gain: float32 [7168], P('dev'), may hold values from 0.1 to 1.9
- router: float32 [7168, 16], P('dev'), may hold values from -0.0625 to 0.0625
- routes: int32 [256, 8], P(('sec', 'grp')), may hold values from 0 to 15, as said below
- slots: int32 [256, 8], P(('sec', 'grp')), may hold values from 0 to 7, as said below
- w_gateup: bfloat16 [16, 7168, 2, 2048], P('grp', 'dev', None, 'sec'), may hold values from -0.0625 to 0.0625
- w_down: bfloat16 [16, 2048, 7168], P('grp', 'sec', 'dev'), may hold values from -0.125 to 0.125
Outputs:
- layer_out: bfloat16 [256, 7168], P(('sec', 'grp'), 'dev')
Inputs may be any that keep to these rules, and one draw needn't show every extreme that they name: `routes`: each row names 8 different experts; one expert is named by every row. Within each aligned block of 8 rows, the routes that name one expert hold the slots 0, 1, ... up to their number less one, each once.
All inputs are finite; a program needn't handle non-finite values.
Results may differ from a plain program's by a relative error of at most 0.033.
Values may be sent and summed in bfloat16 or wider, within the bound.
No kernel may reach another device: no remote copies, remote signals or barrier semaphores. Data moves between devices by JAX's collectives and lax.ppermute only.
A program may use at most 64 MiB of HBM per device.

v0:
```python
import jax
import jax.numpy as jnp
from jax import lax
from jax.sharding import PartitionSpec as P

score_scale = 0.07216878364870323
route_scale = 2.5
norm_eps = 1e-06
masked_floor = -1e30


def merged_2(value, axis, join):
    gathered = jax.tree.map(
        lambda a, kind: lax.all_gather(a.astype(kind), axis),
        value,
        (jnp.bfloat16, jnp.bfloat16, jnp.bfloat16),
    )

    def take(source):
        return jax.tree.map(
            lambda a, own: lax.dynamic_index_in_dim(a, source, 0, False).astype(own.dtype),
            gathered,
            value,
        )

    return lax.fori_loop(
        1, lax.axis_size(axis), lambda source, state: join(state, take(source)), take(0)
    )


def join_parts(former, latter):
    top_former, mass_former, weighted_former = former
    top_latter, mass_latter, weighted_latter = latter
    top_both = jnp.maximum(top_former, top_latter)
    factor_former = jnp.exp(top_former - top_both)
    factor_latter = jnp.exp(top_latter - top_both)
    return (
        top_both,
        mass_former * factor_former + mass_latter * factor_latter,
        weighted_former * factor_former[..., None] + weighted_latter * factor_latter[..., None],
    )


def body(
    q_latent,
    q_rope,
    cache_latent,
    cache_rope,
    lengths,
    w_uv,
    w_out,
    resid,
    norm_gain,
    router,
    routes,
    slots,
    w_gateup,
    w_down,
):
    sections = lax.axis_size("sec")
    groups = lax.axis_size("grp")
    members = lax.axis_size("dev")
    section = lax.axis_index("sec")
    row_count, head_total, latent = q_latent.shape
    hist_local = cache_latent.shape[1]
    rope_width = cache_rope.shape[1]
    half_heads = head_total // sections
    head_block = w_uv.shape[0]
    rope_query = q_rope.reshape(row_count, head_total, rope_width)
    scores = (
        jnp.einsum("rhc,rpc->rhp", q_latent, cache_latent, preferred_element_type=jnp.float32)
        + jnp.einsum("rhj,rjp->rhp", rope_query, cache_rope, preferred_element_type=jnp.float32)
    ) * score_scale
    positions = section * hist_local + jnp.arange(hist_local, dtype=jnp.int32)
    usable = (positions[None, :] < lengths[:, None])[:, None, :]
    masked = jnp.where(usable, scores, masked_floor)
    top_score = jnp.max(masked, axis=-1)
    expon = jnp.where(usable, jnp.exp(masked - top_score[..., None]), 0.0)
    mass_sum = jnp.sum(expon, axis=-1)
    weighted = jnp.einsum(
        "rhp,rpc->rhc", expon.astype(jnp.bfloat16), cache_latent, preferred_element_type=jnp.float32
    )
    mine_start = section * half_heads
    merged = merged_2((top_score, mass_sum, weighted), "sec", join_parts)
    top_mine, mass_mine, weighted_mine = [
        lax.dynamic_slice_in_dim(quantity, mine_start, half_heads, 1) for quantity in merged
    ]
    latent_out = (weighted_mine / mass_mine[..., None]).astype(jnp.bfloat16)
    outgoing_heads = latent_out.reshape(row_count, groups, head_block, latent)
    arrived = lax.all_to_all(outgoing_heads, "grp", split_axis=1, concat_axis=0, tiled=True)
    arrived = arrived.reshape(groups * row_count, head_block, latent)
    values = jnp.einsum("nhc,hcv->nhv", arrived, w_uv, preferred_element_type=jnp.float32).astype(
        jnp.bfloat16
    )
    width_heads = head_block * w_uv.shape[2]
    values = values.reshape(groups * row_count, width_heads)
    gathered = lax.all_gather(values, "dev", axis=0, tiled=True)
    natural = gathered.reshape(members, groups, row_count, width_heads).transpose(1, 0, 2, 3)
    natural = natural.reshape(members * groups * row_count, width_heads)
    block_rows = resid.shape[0]
    attention = lax.psum_scatter(
        jnp.dot(natural, w_out, preferred_element_type=jnp.float32).astype(jnp.bfloat16),
        ("sec", "grp"),
        scatter_dimension=0,
        tiled=True,
    ).astype(jnp.float32)
    hidden_state = resid.astype(jnp.float32) + attention
    gained = hidden_state * norm_gain
    square_sum = jnp.sum(hidden_state * hidden_state, axis=-1)
    router_part = jnp.dot(gained, router, precision=lax.Precision.HIGHEST)
    square_total, logit_total = lax.psum((square_sum, router_part), "dev")
    model_width = norm_gain.shape[0] * members
    inverse_rms = lax.rsqrt(square_total / model_width + norm_eps)
    logits = logit_total * inverse_rms[:, None]
    normed = (gained * inverse_rms[:, None]).astype(jnp.bfloat16)
    expert_total = router.shape[1]
    capacity = max(2, 3 * block_rows // 4)
    expert_ids = jnp.arange(expert_total, dtype=jnp.int32)
    chosen_mask = routes[:, :, None] == expert_ids[None, None, :]
    sigmoid_scores = jax.nn.sigmoid(logits)
    picked = jnp.sum(jnp.where(chosen_mask, sigmoid_scores[:, None, :], 0.0), axis=-1)
    route_weight = route_scale * picked / jnp.sum(picked, axis=-1, keepdims=True)
    kept = slots < capacity
    route_weight = jnp.where(kept, route_weight, 0.0)
    slot_index = routes * capacity + slots
    slot_ids = jnp.arange(expert_total * capacity, dtype=jnp.int32)
    placement_matrix = jnp.any(
        (slot_index[:, :, None] == slot_ids[None, None, :]) & kept[:, :, None], axis=1
    ).astype(jnp.bfloat16)
    width_local = normed.shape[1]
    buffer = jnp.einsum("be,bd->ed", placement_matrix, normed, preferred_element_type=jnp.float32)
    buffer = buffer.astype(jnp.bfloat16).reshape(expert_total, capacity, width_local)
    received = lax.all_to_all(buffer, "grp", split_axis=0, concat_axis=1, tiled=True)
    received = lax.all_gather(received, "sec", axis=1, tiled=True)
    incoming_rows = received[0]
    padded_rows = incoming_rows.shape[0]
    gate_weights = w_gateup[0]
    partial_gate = jnp.einsum(
        "pd,dtf->ptf", incoming_rows, gate_weights, preferred_element_type=jnp.float32
    )
    gate_total = lax.psum(partial_gate.astype(jnp.bfloat16), "dev").astype(jnp.float32)
    activated = (jax.nn.silu(gate_total[:, 0]) * gate_total[:, 1]).astype(jnp.bfloat16)
    down_part = jnp.dot(activated, w_down[0], preferred_element_type=jnp.float32)
    down_total = lax.psum_scatter(
        down_part.reshape(sections, padded_rows // sections, width_local).astype(jnp.bfloat16),
        "sec",
        scatter_dimension=0,
        tiled=True,
    )
    expert_rows = down_total.reshape(groups, capacity, width_local)
    returned = lax.all_to_all(expert_rows, "grp", split_axis=0, concat_axis=0, tiled=True)
    returned = returned.reshape(expert_total * capacity, width_local)
    safe_index = jnp.where(kept, slot_index, 0)
    fetched = returned[safe_index]
    mixture = jnp.sum(route_weight[:, :, None] * fetched.astype(jnp.float32), axis=1)
    return (hidden_state + mixture).astype(jnp.bfloat16)


def solution(mesh):
    in_specs = (
        P(("grp", "dev"), None, None),
        P(("grp", "dev"), None),
        P(("grp", "dev"), "sec", None),
        P(("grp", "dev"), None, "sec"),
        P(("grp", "dev")),
        P(("sec", "grp"), None, None),
        P(("sec", "grp"), "dev"),
        P(("sec", "grp"), "dev"),
        P("dev"),
        P("dev", None),
        P(("sec", "grp"), None),
        P(("sec", "grp"), None),
        P("grp", "dev", None, "sec"),
        P("grp", "sec", "dev"),
    )
    out_specs = P(("sec", "grp"), "dev")
    return jax.shard_map(body, mesh=mesh, in_specs=in_specs, out_specs=out_specs, check_vma=False)
```

profile of v0, /device:TPU:1, one launch (start us, length us, event | category | flops | bytes accessed | tf_op | source)
XLA Modules:
  0.0 402.9 jit_solution(10967352460992047660)
XLA Ops:
  7.3 0.9 reduce.5
  8.3 1.1 fusion.23
  9.4 1.9 fusion.46
  12.0 8.5 %all-gather.3 = bf16[2,1,128]{2,1,0:T(2,128)(2,1)S(1)} all-gather(bf16[1,1,128]{2,1,0:T(2,128)(2,1)S(1)} %convert_bitcast_fusion.1), channel_id=3, replica_groups=mesh['sec'=2,'grp'=16,'dev'=16] {'sec'}, dimensions={0}, use_global_device_ids=true | all-gather | bytes 768 | tf_op jit(solution)/shard_map/all_gather | solution.py:14
  20.4 1.8 all-gather.4
  22.4 2.0 all-gather
  24.6 12.8 %all_to_all.26 = bf16[1,16,4,512]{3,2,0,1:T(4,128)(2,1)S(1)} all-to-all(bf16[1,16,4,512]{3,2,0,1:T(4,128)(2,1)S(1)} %bitcast.106), channel_id=1, replica_groups=mesh['sec'=2,'grp'=16,'dev'=16] {'grp'}, dimensions={1} | all-to-all | bytes 131072 | tf_op jit(solution)/shard_map/all_to_all | solution.py:90
  37.6 32.9 %all_gather.24 = bf16[256,512]{1,0:T(8,128)(2,1)S(1)} all-gather(bf16[16,512]{1,0:T(8,128)(2,1)S(1)} %bitcast.107), channel_id=1, replica_groups=mesh['sec'=2,'grp'=16,'dev'=16] {'dev'}, dimensions={0}, use_global_device_ids=true | all-gather | bytes 278528 | tf_op jit(solution)/shard_map/all_gather | solution.py:97
  70.6 1.0 convolution_convert_fusion
  71.7 92.9 %reduce-scatter.3.cloned.1.call-done = bf16[8,448]{1,0:T(8,128)(2,1)} async-done(((bf16[256,448]{1,0:T(8,128)(2,1)}), bf16[8,448]{1,0:T(8,128)(2,1)}) %reduce-scatter.3.cloned.1.call-update) | async-done | bytes 7184 | tf_op jit(solution)/shard_map/reduce_scatter | solution.py:101
  164.7 0.8 fusion.30
  165.5 0.8 multiply_reduce_fusion
  166.3 28.1 %all-reduce = (f32[8]{0:T(128)S(1)}, f32[8,16]{1,0:T(8,128)S(1)}) all-reduce(f32[8]{0:T(128)S(1)} %multiply_reduce_fusion, f32[8,16]{1,0:T(8,128)S(1)} %fusion.30), channel_id=1, replica_groups=mesh['sec'=2,'grp'=16,'dev'=16] {'dev'}, use_global_device_ids=true, to_apply=%region_5.6 | all-reduce | flops 136 | bytes 1088 | tf_op jit(solution)/shard_map/psum | solution.py:111
  195.0 1.0 convolution_convert_fusion.3
  196.0 14.3 %all_to_all.27 = bf16[16,6,448]{2,1,0:T(8,128)(2,1)S(1)} all-to-all(bf16[16,6,448]{2,1,0:T(8,128)(2,1)S(1)} %reshape.324), channel_id=1, replica_groups=mesh['sec'=2,'grp'=16,'dev'=16] {'grp'}, dimensions={0} | all-to-all | bytes 172032 | tf_op jit(solution)/shard_map/all_to_all | solution.py:133
  210.4 13.1 %all_gather.25 = bf16[1,192,448]{2,1,0:T(8,128)(2,1)S(1)} all-gather(bf16[1,96,448]{2,1,0:T(8,128)(2,1)S(1)} %all_to_all.10), channel_id=1, replica_groups=mesh['sec'=2,'grp'=16,'dev'=16] {'sec'}, dimensions={1}, use_global_device_ids=true | all-gather | bytes 258048 | tf_op jit(solution)/shard_map/all_gather | solution.py:134
  223.5 1.7 fusion.2
  225.3 122.5 %all-reduce.3.cloned.1.call-done = bf16[192,2,1024]{2,0,1:T(8,128)(2,1)} async-done(((bf16[192,2,1024]{2,0,1:T(8,128)(2,1)}), bf16[192,2,1024]{2,0,1:T(8,128)(2,1)}) %all-reduce.3.cloned.1.call-update) | async-done | bytes 786448 | tf_op jit(solution)/shard_map/psum | solution.py:141
  347.8 1.3 convert_element_type.231
  349.4 1.1 convolution_convert_fusion.1
  350.5 25.5 %reduce-scatter.5.cloned.1.call-done = bf16[1,96,448]{2,1,0:T(8,128)(2,1)} async-done(((bf16[2,96,448]{2,1,0:T(8,128)(2,1)}), bf16[1,96,448]{2,1,0:T(8,128)(2,1)}) %reduce-scatter.5.cloned.1.call-update) | async-done | bytes 86032 | tf_op jit(solution)/shard_map/reduce_scatter | solution.py:144
  376.0 1.6 reshape.325
  377.5 8.0 %all-to-all-start.2 = ((bf16[16,6,448]{2,1,0:T(8,128)(2,1)}), bf16[16,6,448]{2,1,0:T(8,128)(2,1)S(1)}, u32[]{:S(2)}, u32[]{:S(2)}) async-start(bf16[16,6,448]{2,1,0:T(8,128)(2,1)} %reshape.325), calls=%async_computation.4 | async-start | bytes 262144 | tf_op jit(solution)/shard_map/all_to_all | solution.py:151
  385.6 9.2 %all-to-all-done.2 = bf16[16,6,448]{2,1,0:T(8,128)(2,1)S(1)} async-done(((bf16[16,6,448]{2,1,0:T(8,128)(2,1)}), bf16[16,6,448]{2,1,0:T(8,128)(2,1)S(1)}, u32[]{:S(2)}, u32[]{:S(2)}) %all-to-all-start.2) | async-done | bytes 86048 | tf_op jit(solution)/shard_map/all_to_all | solution.py:151
  (59 shorter events, 4.0 us)
Async XLA Ops:
  6.5 217.0 %copy-start = (bf16[1,448,2,1024]{3,2,1,0:T(2,128)(2,1)S(1)}, bf16[1,448,2,1024]{3,2,1,0:T(2,128)(2,1)}, u32[]{:S(2)}) copy-start(bf16[1,448,2,1024]{3,2,1,0:T(2,128)(2,1)} %param.26) | copy-start | bytes 5505028
  6.5 5.0 %copy-start.1 = (bf16[1,1024,512]{2,1,0:T(8,128)(2,1)S(1)}, bf16[1,1024,512]{2,1,0:T(8,128)(2,1)}, u32[]{:S(2)}) copy-start(bf16[1,1024,512]{2,1,0:T(8,128)(2,1)} %param.16) | copy-start | bytes 3145732
  6.5 158.1 %reduce-scatter.3.cloned.1.call-start = ((), (), s32[]{:S(2)}) async-start(), calls=%async_computation.5 | async-start | bytes 270336 | tf_op jit(solution)/shard_map/reduce_scatter | solution.py:101
  11.3 26.1 %copy-start.3 = (bf16[4,512,128]{2,1,0:T(8,128)(2,1)S(1)}, bf16[4,512,128]{2,1,0:T(8,128)(2,1)}, u32[]{:S(2)}) copy-start(bf16[4,512,128]{2,1,0:T(8,128)(2,1)} %param.19) | copy-start | bytes 1572868
  11.9 58.7 %copy-start.4 = (bf16[512,448]{0,1:T(8,128)(2,1)S(1)}, bf16[512,448]{0,1:T(8,128)(2,1)}, u32[]{:S(2)}) copy-start(bf16[512,448]{0,1:T(8,128)(2,1)} %param.20) | copy-start | bytes 1376260
  24.4 140.2 %copy-start.5 = (bf16[8,448]{1,0:T(8,128)(2,1)S(1)}, bf16[8,448]{1,0:T(8,128)(2,1)}, u32[]{:S(2)}) copy-start(bf16[8,448]{1,0:T(8,128)(2,1)} %param.21) | copy-start | bytes 21508
  24.4 140.2 %copy-start.7 = (f32[448,16]{0,1:T(8,128)S(1)}, f32[448,16]{0,1:T(8,128)}, u32[]{:S(2)}) copy-start(f32[448,16]{0,1:T(8,128)} %param.23) | copy-start | bytes 86020
  24.4 140.2 %copy-start.10 = (f32[448]{0:T(512)S(1)}, f32[448]{0:T(512)}, u32[]{:S(2)}) copy-start(f32[448]{0:T(512)} %param.22) | copy-start | bytes 5380
  24.4 170.1 %copy-start.8 = (s32[8,8]{1,0:T(8,128)S(1)}, s32[8,8]{1,0:T(8,128)}, u32[]{:S(2)}) copy-start(s32[8,8]{1,0:T(8,128)} %param.24) | copy-start | bytes 772
  24.4 170.3 %copy-start.9 = (s32[8,8]{1,0:T(8,128)S(1)}, s32[8,8]{1,0:T(8,128)}, u32[]{:S(2)}) copy-start(s32[8,8]{1,0:T(8,128)} %param.25) | copy-start | bytes 772
  71.7 276.1 %all-reduce.3.cloned.1.call-start = ((), (), s32[]{:S(2)}) async-start(), calls=%async_computation.6 | async-start | bytes 1572864 | tf_op jit(solution)/shard_map/psum | solution.py:141
  225.2 124.1 %copy-start.2 = (bf16[1,1024,448]{1,2,0:T(8,128)(2,1)S(1)}, bf16[1,1024,448]{1,2,0:T(8,128)(2,1)}, u32[]{:S(2)}) copy-start(bf16[1,1024,448]{1,2,0:T(8,128)(2,1)} %param.27) | copy-start | bytes 2752516
  225.2 150.8 %reduce-scatter.5.cloned.1.call-start = ((), (), s32[]{:S(2)}) async-start(), calls=%async_computation.7 | async-start | bytes 294912 | tf_op jit(solution)/shard_map/reduce_scatter | solution.py:144
  349.3 46.4 %copy-start.6 = (bf16[8,448]{1,0:T(8,128)(2,1)S(1)}, bf16[8,448]{1,0:T(8,128)(2,1)}, u32[]{:S(2)}) copy-start(bf16[8,448]{1,0:T(8,128)(2,1)} %reduce-scatter.3.cloned.1.call-done) | copy-start | bytes 21508
  377.5 17.3 %all-to-all-start.2 = ((bf16[16,6,448]{2,1,0:T(8,128)(2,1)}), bf16[16,6,448]{2,1,0:T(8,128)(2,1)S(1)}, u32[]{:S(2)}, u32[]{:S(2)}) async-start(bf16[16,6,448]{2,1,0:T(8,128)(2,1)} %reshape.325), calls=%async_computation.4 | async-start | bytes 262144 | tf_op jit(solution)/shard_map/all_to_all | solution.py:151
Sparse Core Ops, SparseCore 0:
  71.8 92.8 reduce-scatter.2
  225.3 122.4 all-reduce.2
  350.8 25.1 reduce-scatter.4
where the time goes:
time: 404 us; the launch traced here: 403 us
  waiting for transfers between devices  250 us (62%)
  blocking collectives  113 us (28%)
  between operations  14.1 us (3%)
  matrix products  9.13 us (2%)
  starting transfers between devices  8.08 us (2%)
  other arithmetic  4.83 us (1%)
    psum x1, waiting for transfers between devices, body(): lax.psum(partial_gate.astype(jnp.bfloat16), 'dev').astype(jnp.float32)  123 us
    reduce_scatter x1, waiting for transfers between devices, body(): lax.psum_scatter(jnp.dot(natural, w_out, preferred_element_type=jnp.float...  92.9 us
    all_gather x1, blocking collectives, body(): gathered = lax.all_gather(values, 'dev', axis=0, tiled=True)  32.9 us
    psum x1, blocking collectives, body(): square_total, logit_total = lax.psum((square_sum, router_part), 'dev')  28.1 us
    reduce_scatter x1, waiting for transfers between devices, body(): lax.psum_scatter(down_part.reshape(sections, padded_rows // sections, wid...  25.5 us
    all_to_all x1, blocking collectives, body(): lax.all_to_all(buffer, 'grp', split_axis=0, concat_axis=1, tiled=True)  14.3 us
    all_gather x1, blocking collectives, body(): received = lax.all_gather(received, 'sec', axis=1, tiled=True)  13.1 us
    all_to_all x1, blocking collectives, body(): lax.all_to_all(outgoing_heads, 'grp', split_axis=1, concat_axis=0, tiled=...  12.8 us
  transfers between devices with their start and end apart: 4, of which 4 were waited for; matrix products, arithmetic and copies ran while one was open for 0% of the time, Pallas kernels for 0%

commit v1 on v0

--- a/solution.py
+++ b/solution.py
@@ -131,7 +131,9 @@
     buffer = jnp.einsum("be,bd->ed", placement_matrix, normed, preferred_element_type=jnp.float32)
     buffer = buffer.astype(jnp.bfloat16).reshape(expert_total, capacity, width_local)
     received = lax.all_to_all(buffer, "grp", split_axis=0, concat_axis=1, tiled=True)
-    received = lax.all_gather(received, "sec", axis=1, tiled=True)
+    received = jnp.concatenate(
+        lax.all_to_all(jnp.stack([received] * lax.axis_size("sec")), "sec", 0, 0), axis=1
+    )
     incoming_rows = received[0]
     padded_rows = incoming_rows.shape[0]
     gate_weights = w_gateup[0]

time: 404 us -> 405 us (level)
    all_to_all x0 -> x1, blocking collectives: none -> 15.1 us  [body(): lax.all_to_all(jnp.stack([received] * lax.axis_size('sec')), 'sec', 0, 0)]
    all_gather x1 -> x0, blocking collectives: 13.1 us -> none  [body(): received = lax.all_gather(received, 'sec', axis=1, tiled=True)]
where the time goes in v1:
time: 405 us
  waiting for transfers between devices  250 us (62%)
  blocking collectives  115 us (28%)
  between operations  14.1 us (3%)
  matrix products  9.13 us (2%)
  starting transfers between devices  8.08 us (2%)
  other arithmetic  4.85 us (1%)
    psum x1, waiting for transfers between devices, body(): lax.psum(partial_gate.astype(jnp.bfloat16), 'dev').astype(jnp.float32)  122 us
    reduce_scatter x1, waiting for transfers between devices, body(): lax.psum_scatter(jnp.dot(natural, w_out, preferred_element_type=jnp.float...  92.9 us
    all_gather x1, blocking collectives, body(): gathered = lax.all_gather(values, 'dev', axis=0, tiled=True)  32.9 us
    psum x1, blocking collectives, body(): square_total, logit_total = lax.psum((square_sum, router_part), 'dev')  28.1 us
    reduce_scatter x1, waiting for transfers between devices, body(): lax.psum_scatter(down_part.reshape(sections, padded_rows // sections, wid...  25.5 us
    all_to_all x1, blocking collectives, body(): lax.all_to_all(jnp.stack([received] * lax.axis_size('sec')), 'sec', 0, 0)  15.1 us
    all_to_all x1, blocking collectives, body(): lax.all_to_all(buffer, 'grp', split_axis=0, concat_axis=1, tiled=True)  14.3 us
    all_to_all x1, blocking collectives, body(): lax.all_to_all(outgoing_heads, 'grp', split_axis=1, concat_axis=0, tiled=...  12.8 us
  transfers between devices with their start and end apart: 4, of which 4 were waited for; matrix products, arithmetic and copies ran while one was open for 0% of the time, Pallas kernels for 0%

profile of v1, /device:TPU:1, one launch (start us, length us, event | category | flops | bytes accessed | tf_op | source)
XLA Modules:
  0.0 404.7 jit_solution(14552817866199936247)
XLA Ops:
  7.3 0.9 reduce.5
  8.3 1.1 fusion.22
  9.4 1.9 fusion.45
  12.0 8.5 %all-gather.3 = bf16[2,1,128]{2,1,0:T(2,128)(2,1)S(1)} all-gather(bf16[1,1,128]{2,1,0:T(2,128)(2,1)S(1)} %convert_bitcast_fusion.1), channel_id=3, replica_groups=mesh['sec'=2,'grp'=16,'dev'=16] {'sec'}, dimensions={0}, use_global_device_ids=true | all-gather | bytes 768 | tf_op jit(solution)/shard_map/all_gather | solution.py:14
  20.4 1.8 all-gather.4
  22.4 2.0 all-gather
  24.6 12.8 %all_to_all.28 = bf16[1,16,4,512]{3,2,0,1:T(4,128)(2,1)S(1)} all-to-all(bf16[1,16,4,512]{3,2,0,1:T(4,128)(2,1)S(1)} %bitcast.106), channel_id=1, replica_groups=mesh['sec'=2,'grp'=16,'dev'=16] {'grp'}, dimensions={1} | all-to-all | bytes 131072 | tf_op jit(solution)/shard_map/all_to_all | solution.py:90
  37.6 32.9 %all_gather.21 = bf16[256,512]{1,0:T(8,128)(2,1)S(1)} all-gather(bf16[16,512]{1,0:T(8,128)(2,1)S(1)} %bitcast.108), channel_id=1, replica_groups=mesh['sec'=2,'grp'=16,'dev'=16] {'dev'}, dimensions={0}, use_global_device_ids=true | all-gather | bytes 278528 | tf_op jit(solution)/shard_map/all_gather | solution.py:97
  70.6 1.0 convolution_convert_fusion
  71.7 92.9 %reduce-scatter.3.cloned.1.call-done = bf16[8,448]{1,0:T(8,128)(2,1)} async-done(((bf16[256,448]{1,0:T(8,128)(2,1)}), bf16[8,448]{1,0:T(8,128)(2,1)}) %reduce-scatter.3.cloned.1.call-update) | async-done | bytes 7184 | tf_op jit(solution)/shard_map/reduce_scatter | solution.py:101
  164.7 0.8 fusion.29
  165.5 0.8 multiply_reduce_fusion
  166.3 28.1 %all-reduce = (f32[8]{0:T(128)S(1)}, f32[8,16]{1,0:T(8,128)S(1)}) all-reduce(f32[8]{0:T(128)S(1)} %multiply_reduce_fusion, f32[8,16]{1,0:T(8,128)S(1)} %fusion.29), channel_id=1, replica_groups=mesh['sec'=2,'grp'=16,'dev'=16] {'dev'}, use_global_device_ids=true, to_apply=%region_5.6 | all-reduce | flops 136 | bytes 1088 | tf_op jit(solution)/shard_map/psum | solution.py:111
  195.0 1.0 convolution_convert_fusion.3
  196.0 14.3 %all_to_all.29 = bf16[16,6,448]{2,1,0:T(8,128)(2,1)S(1)} all-to-all(bf16[16,6,448]{2,1,0:T(8,128)(2,1)S(1)} %reshape.325), channel_id=1, replica_groups=mesh['sec'=2,'grp'=16,'dev'=16] {'grp'}, dimensions={0} | all-to-all | bytes 172032 | tf_op jit(solution)/shard_map/all_to_all | solution.py:133
  210.4 15.1 %all_to_all.30 = bf16[2,1,96,448]{3,2,1,0:T(8,128)(2,1)S(1)} all-to-all(bf16[2,1,96,448]{3,2,1,0:T(8,128)(2,1)S(1)} %pad_maximum_fusion), channel_id=1, replica_groups=mesh['sec'=2,'grp'=16,'dev'=16] {'sec'}, dimensions={0} | all-to-all | bytes 344064 | tf_op jit(solution)/shard_map/all_to_all | solution.py:135
  225.5 1.7 fusion.2
  227.2 122.3 %all-reduce.3.cloned.1.call-done = bf16[192,2,1024]{2,0,1:T(8,128)(2,1)} async-done(((bf16[192,2,1024]{2,0,1:T(8,128)(2,1)}), bf16[192,2,1024]{2,0,1:T(8,128)(2,1)}) %all-reduce.3.cloned.1.call-update) | async-done | bytes 786448 | tf_op jit(solution)/shard_map/psum | solution.py:143
  349.6 1.3 convert_element_type.231
  351.1 1.1 convolution_convert_fusion.1
  352.3 25.5 %reduce-scatter.5.cloned.1.call-done = bf16[1,96,448]{2,1,0:T(8,128)(2,1)} async-done(((bf16[2,96,448]{2,1,0:T(8,128)(2,1)}), bf16[1,96,448]{2,1,0:T(8,128)(2,1)}) %reduce-scatter.5.cloned.1.call-update) | async-done | bytes 86032 | tf_op jit(solution)/shard_map/reduce_scatter | solution.py:146
  377.7 1.6 reshape.326
  379.3 8.0 %all-to-all-start.3 = ((bf16[16,6,448]{2,1,0:T(8,128)(2,1)}), bf16[16,6,448]{2,1,0:T(8,128)(2,1)S(1)}, u32[]{:S(2)}, u32[]{:S(2)}) async-start(bf16[16,6,448]{2,1,0:T(8,128)(2,1)} %reshape.326), calls=%async_computation.5 | async-start | bytes 262144 | tf_op jit(solution)/shard_map/all_to_all | solution.py:153
  387.4 9.2 %all-to-all-done.3 = bf16[16,6,448]{2,1,0:T(8,128)(2,1)S(1)} async-done(((bf16[16,6,448]{2,1,0:T(8,128)(2,1)}), bf16[16,6,448]{2,1,0:T(8,128)(2,1)S(1)}, u32[]{:S(2)}, u32[]{:S(2)}) %all-to-all-start.3) | async-done | bytes 86048 | tf_op jit(solution)/shard_map/all_to_all | solution.py:153
  (60 shorter events, 4.0 us)
Async XLA Ops:
  6.5 218.9 %copy-start = (bf16[1,448,2,1024]{3,2,1,0:T(2,128)(2,1)S(1)}, bf16[1,448,2,1024]{3,2,1,0:T(2,128)(2,1)}, u32[]{:S(2)}) copy-start(bf16[1,448,2,1024]{3,2,1,0:T(2,128)(2,1)} %param.26) | copy-start | bytes 5505028
  6.5 5.0 %copy-start.1 = (bf16[1,1024,512]{2,1,0:T(8,128)(2,1)S(1)}, bf16[1,1024,512]{2,1,0:T(8,128)(2,1)}, u32[]{:S(2)}) copy-start(bf16[1,1024,512]{2,1,0:T(8,128)(2,1)} %param.16) | copy-start | bytes 3145732
  6.5 158.1 %reduce-scatter.3.cloned.1.call-start = ((), (), s32[]{:S(2)}) async-start(), calls=%async_computation.6 | async-start | bytes 270336 | tf_op jit(solution)/shard_map/reduce_scatter | solution.py:101
  11.3 26.1 %copy-start.3 = (bf16[4,512,128]{2,1,0:T(8,128)(2,1)S(1)}, bf16[4,512,128]{2,1,0:T(8,128)(2,1)}, u32[]{:S(2)}) copy-start(bf16[4,512,128]{2,1,0:T(8,128)(2,1)} %param.19) | copy-start | bytes 1572868
  11.9 58.7 %copy-start.4 = (bf16[512,448]{0,1:T(8,128)(2,1)S(1)}, bf16[512,448]{0,1:T(8,128)(2,1)}, u32[]{:S(2)}) copy-start(bf16[512,448]{0,1:T(8,128)(2,1)} %param.20) | copy-start | bytes 1376260
  24.4 140.2 %copy-start.5 = (bf16[8,448]{1,0:T(8,128)(2,1)S(1)}, bf16[8,448]{1,0:T(8,128)(2,1)}, u32[]{:S(2)}) copy-start(bf16[8,448]{1,0:T(8,128)(2,1)} %param.21) | copy-start | bytes 21508
  24.4 140.2 %copy-start.7 = (f32[448,16]{0,1:T(8,128)S(1)}, f32[448,16]{0,1:T(8,128)}, u32[]{:S(2)}) copy-start(f32[448,16]{0,1:T(8,128)} %param.23) | copy-start | bytes 86020
  24.4 140.2 %copy-start.10 = (f32[448]{0:T(512)S(1)}, f32[448]{0:T(512)}, u32[]{:S(2)}) copy-start(f32[448]{0:T(512)} %param.22) | copy-start | bytes 5380
  24.4 170.1 %copy-start.8 = (s32[8,8]{1,0:T(8,128)S(1)}, s32[8,8]{1,0:T(8,128)}, u32[]{:S(2)}) copy-start(s32[8,8]{1,0:T(8,128)} %param.24) | copy-start | bytes 772
  24.4 170.3 %copy-start.9 = (s32[8,8]{1,0:T(8,128)S(1)}, s32[8,8]{1,0:T(8,128)}, u32[]{:S(2)}) copy-start(s32[8,8]{1,0:T(8,128)} %param.25) | copy-start | bytes 772
  71.7 277.9 %all-reduce.3.cloned.1.call-start = ((), (), s32[]{:S(2)}) async-start(), calls=%async_computation.7 | async-start | bytes 1572864 | tf_op jit(solution)/shard_map/psum | solution.py:143
  227.2 123.9 %copy-start.2 = (bf16[1,1024,448]{1,2,0:T(8,128)(2,1)S(1)}, bf16[1,1024,448]{1,2,0:T(8,128)(2,1)}, u32[]{:S(2)}) copy-start(bf16[1,1024,448]{1,2,0:T(8,128)(2,1)} %param.27) | copy-start | bytes 2752516
  227.2 150.6 %reduce-scatter.5.cloned.1.call-start = ((), (), s32[]{:S(2)}) async-start(), calls=%async_computation.8 | async-start | bytes 294912 | tf_op jit(solution)/shard_map/reduce_scatter | solution.py:146
  351.1 46.4 %copy-start.6 = (bf16[8,448]{1,0:T(8,128)(2,1)S(1)}, bf16[8,448]{1,0:T(8,128)(2,1)}, u32[]{:S(2)}) copy-start(bf16[8,448]{1,0:T(8,128)(2,1)} %reduce-scatter.3.cloned.1.call-done) | copy-start | bytes 21508
  379.3 17.3 %all-to-all-start.3 = ((bf16[16,6,448]{2,1,0:T(8,128)(2,1)}), bf16[16,6,448]{2,1,0:T(8,128)(2,1)S(1)}, u32[]{:S(2)}, u32[]{:S(2)}) async-start(bf16[16,6,448]{2,1,0:T(8,128)(2,1)} %reshape.326), calls=%async_computation.5 | async-start | bytes 262144 | tf_op jit(solution)/shard_map/all_to_all | solution.py:153
Sparse Core Ops, SparseCore 0:
  71.8 92.8 reduce-scatter.2
  227.3 122.2 all-reduce.2
  352.6 25.1 reduce-scatter.4
